TPU v7x, 256 devices: a whole 4x4x8 slice. The times are simulated.
256 devices in a mesh: bucket: 64 (over x, z, core), row: 4 (over y).
Axes of the slice: x: 4, y: 4, z: 8, core: 2. Of those that a mesh axis runs over, the one named last changes fastest.
Arguments:
- entities: float32 [131072, 400], P(('bucket', 'row')), may hold values from -21.6 to 21.6
- relations: float32 [1300, 400], replicated, may hold values from -1.35 to 1.35
- touch_owner: int32 [256, 64], P(('bucket', 'row')), may hold values from 0 to 63, as said below
- touch_block: int32 [256, 64], P(('bucket', 'row')), may hold values from 0 to 3
- head_ids: int32 [262144], P(('bucket', 'row')), may hold values from 0 to 8191
- rel_ids: int32 [262144], P(('bucket', 'row')), may hold values from 0 to 1299
- tail_ids: int32 [262144], P(('bucket', 'row')), may hold values from 0 to 8191
- neg_tail: int32 [256, 100], P(('bucket', 'row')), may hold values from 0 to 8191
- neg_head: int32 [256, 100], P(('bucket', 'row')), may hold values from 0 to 8191
Outputs:
- entity_grad: float32 [131072, 400], P(('bucket', 'row'))
- relation_grad: float32 [1300, 400], replicated
Inputs may be any that keep to these rules, and one draw needn't show every extreme that they name: `touch_owner`: each row names every bucket index once.
All inputs are finite; a program needn't handle non-finite values.
Results may differ from a plain program's by a relative error of at most 0.0073.
Values may be sent and summed in bfloat16 or wider, within the bound.
A program may use at most 192 MiB of HBM per device.

v0:
```python
import jax
import jax.numpy as jnp
from jax import lax
from jax.sharding import PartitionSpec as P

BLOCK = 128


def side_weights(positive, scores):
    largest = jnp.maximum(positive, jnp.max(scores, axis=1))
    own_term = jnp.exp(positive - largest)
    others = jnp.exp(scores - largest[:, None])
    total = own_term + jnp.sum(others, axis=1)
    return (own_term / total - 1.0, others / total[:, None])


def edge_block_grads(buffer, relations, head_ids, rel_ids, tail_ids, neg_tail, neg_head):
    middle = relations.shape[1] // 2
    head_rows = jnp.take(buffer, head_ids, axis=0).astype(jnp.float32)
    tail_rows = jnp.take(buffer, tail_ids, axis=0).astype(jnp.float32)
    rel_rows = jnp.take(relations, rel_ids, axis=0)
    rel_real, rel_imag = (rel_rows[:, :middle], rel_rows[:, middle:])
    head_real, head_imag = (head_rows[:, :middle], head_rows[:, middle:])
    tail_real, tail_imag = (tail_rows[:, :middle], tail_rows[:, middle:])
    query = jnp.concatenate(
        [head_real * rel_real - head_imag * rel_imag, head_real * rel_imag + head_imag * rel_real],
        axis=1,
    )
    probe = jnp.concatenate(
        [rel_real * tail_real + rel_imag * tail_imag, rel_real * tail_imag - rel_imag * tail_real],
        axis=1,
    )
    positive = jnp.sum(query * tail_rows, axis=1)
    tail_negs = jnp.take(buffer, neg_tail, axis=0)
    head_negs = jnp.take(buffer, neg_head, axis=0)
    query_low = query.astype(jnp.bfloat16)
    probe_low = probe.astype(jnp.bfloat16)
    contract_last = (((1,), (1,)), ((), ()))
    contract_first = (((0,), (0,)), ((), ()))
    tail_scores = lax.dot_general(
        query_low, tail_negs, contract_last, preferred_element_type=jnp.float32
    )
    head_scores = lax.dot_general(
        probe_low, head_negs, contract_last, preferred_element_type=jnp.float32
    )
    tail_coef, tail_weights = side_weights(positive, tail_scores)
    head_coef, head_weights = side_weights(positive, head_scores)
    tail_low = tail_weights.astype(jnp.bfloat16)
    head_low = head_weights.astype(jnp.bfloat16)
    both_coef = (tail_coef + head_coef)[:, None]
    query_grad = both_coef * tail_rows + jnp.dot(
        tail_low, tail_negs, preferred_element_type=jnp.float32
    )
    probe_grad = jnp.dot(head_low, head_negs, preferred_element_type=jnp.float32)
    tail_neg_grad = lax.dot_general(
        tail_low, query_low, contract_first, preferred_element_type=jnp.float32
    )
    head_neg_grad = lax.dot_general(
        head_low, probe_low, contract_first, preferred_element_type=jnp.float32
    )
    qgrad_real, qgrad_imag = (query_grad[:, :middle], query_grad[:, middle:])
    pgrad_real, pgrad_imag = (probe_grad[:, :middle], probe_grad[:, middle:])
    head_grad = jnp.concatenate(
        [
            qgrad_real * rel_real + qgrad_imag * rel_imag,
            qgrad_imag * rel_real - qgrad_real * rel_imag,
        ],
        axis=1,
    )
    tail_grad = both_coef * query + jnp.concatenate(
        [
            pgrad_real * rel_real - pgrad_imag * rel_imag,
            pgrad_real * rel_imag + pgrad_imag * rel_real,
        ],
        axis=1,
    )
    rel_edge_grad = jnp.concatenate(
        [
            qgrad_real * head_real
            + qgrad_imag * head_imag
            + pgrad_real * tail_real
            + pgrad_imag * tail_imag,
            qgrad_imag * head_real
            - qgrad_real * head_imag
            + pgrad_real * tail_imag
            - pgrad_imag * tail_real,
        ],
        axis=1,
    )
    row_ids = jnp.concatenate([head_ids, tail_ids, neg_tail, neg_head])
    row_vals = jnp.concatenate([head_grad, tail_grad, tail_neg_grad, head_neg_grad], axis=0)
    return (row_ids, row_vals, rel_edge_grad)


def device_grads(buffer, relations, head_ids, rel_ids, tail_ids, neg_tail, neg_head):
    blocks_count = neg_tail.shape[0]
    start_zero = (jnp.zeros(buffer.shape, jnp.float32), jnp.zeros(relations.shape, jnp.float32))

    def advance(totals, position):
        row_ids, row_vals, rel_edge_grad = edge_block_grads(
            buffer, relations, head_ids, rel_ids, tail_ids, neg_tail[position], neg_head[position]
        )
        return (
            (totals[0].at[row_ids].add(row_vals), totals[1].at[rel_ids].add(rel_edge_grad)),
            None,
        )

    totals, unused = lax.scan(advance, start_zero, jnp.arange(blocks_count, dtype=jnp.int32))
    return totals


def per_device(
    entities, relations, touch_owner, touch_block, head_ids, rel_ids, tail_ids, neg_tail, neg_head
):
    bucket_count = lax.axis_size("bucket")
    block_rows = BLOCK
    width = entities.shape[1]
    owned = entities.shape[0] // block_rows
    owners = touch_owner[0]
    wanted = touch_block[0]
    touched = owners.shape[0]
    slot_ids = jnp.arange(bucket_count, dtype=jnp.int32)
    matches = owners[:, None] == slot_ids[None, :]
    request = jnp.sum(jnp.where(matches, wanted[:, None] + 1, 0), axis=0) - 1
    incoming = lax.all_to_all(request, "bucket", split_axis=0, concat_axis=0, tiled=True)
    selector = (incoming[:, None] == jnp.arange(owned, dtype=jnp.int32)[None, :]).astype(
        jnp.float32
    )
    owned_flat = entities.reshape(owned, block_rows * width)
    reply = jnp.dot(selector, owned_flat, precision=lax.Precision.HIGHEST).astype(jnp.bfloat16)
    reply = reply.reshape(bucket_count, block_rows, width)
    fetched = lax.all_to_all(reply, "bucket", split_axis=0, concat_axis=0, tiled=True)
    buffer = jnp.take(fetched, owners, axis=0).reshape(touched * block_rows, width)
    buffer_grad, rel_part = device_grads(
        buffer, relations, head_ids, rel_ids, tail_ids, neg_tail, neg_head
    )
    outgoing = jnp.zeros((bucket_count, block_rows, width), jnp.float32)
    outgoing = outgoing.at[owners].set(buffer_grad.reshape(touched, block_rows, width))
    returned = lax.all_to_all(outgoing, "bucket", split_axis=0, concat_axis=0, tiled=True)
    entity_grad = lax.dot_general(
        selector,
        returned.reshape(bucket_count, block_rows * width),
        (((0,), (0,)), ((), ())),
        precision=lax.Precision.HIGHEST,
    )
    entity_grad = entity_grad.reshape(owned * block_rows, width)
    relation_grad = lax.psum(rel_part, ("bucket", "row"))
    return (entity_grad, relation_grad)


def solution(mesh):
    return jax.shard_map(
        per_device,
        mesh=mesh,
        in_specs=(
            P(("bucket", "row"), None),
            P(),
            P(("bucket", "row"), None),
            P(("bucket", "row"), None),
            P(("bucket", "row")),
            P(("bucket", "row")),
            P(("bucket", "row")),
            P(("bucket", "row"), None),
            P(("bucket", "row"), None),
        ),
        out_specs=(P(("bucket", "row"), None), P()),
        check_vma=False,
    )
```

profile of v0, /device:TPU:6, one launch (start us, length us, event | category | flops | bytes accessed | tf_op | source)
XLA Modules:
  0.0 774.7 jit_solution(7517615695962110372)
XLA Ops:
  9.3 12.2 %all-to-all-start = ((s32[64,1,1]{2,1,0:T(1,128)}), s32[64,1,1]{2,1,0:T(1,128)S(1)}, u32[]{:S(2)}, u32[]{:S(2)}) async-start(s32[64,1,1]{2,1,0:T(1,128)} %copy.60), calls=%async_computation | async-start | bytes 65536 | tf_op jit(solution)/shard_map/all_to_all | solution.py:125
  30.2 7.2 convolution_convert_fusion
  37.4 20.5 %reshape.297 = bf16[64,128,400]{2,1,0:T(8,128)(2,1)} reshape(bf16[64,51200]{1,0:T(8,128)(2,1)} %convolution_convert_fusion) | data formatting | bytes 13107200 | tf_op jit(solution)/shard_map/reshape | solution.py:131
  57.9 10.7 %copy.62 = bf16[64,128,400]{1,2,0:T(8,128)(2,1)} copy(bf16[64,128,400]{2,1,0:T(8,128)(2,1)} %reshape.297) | data formatting | bytes 13107200 | tf_op jit(solution)/shard_map/reshape | solution.py:131
  68.6 8.2 %all-to-all-start.1 = ((bf16[64,128,400]{1,2,0:T(8,128)(2,1)}), bf16[64,128,400]{1,2,0:T(8,128)(2,1)}, u32[]{:S(2)}, u32[]{:S(2)}) async-start(bf16[64,128,400]{1,2,0:T(8,128)(2,1)} %copy.62), calls=%async_computation.1 | async-start | bytes 13107200 | tf_op jit(solution)/shard_map/all_to_all | solution.py:132
  87.8 132.9 %all-to-all-done.1 = bf16[64,128,400]{1,2,0:T(8,128)(2,1)} async-done(((bf16[64,128,400]{1,2,0:T(8,128)(2,1)}), bf16[64,128,400]{1,2,0:T(8,128)(2,1)}, u32[]{:S(2)}, u32[]{:S(2)}) %all-to-all-start.1) | async-done | bytes 6553632 | tf_op jit(solution)/shard_map/all_to_all | solution.py:132
  220.8 7.0 gather_fusion
  227.8 10.6 %copy.63 = bf16[64,128,400]{2,1,0:T(8,128)(2,1)} copy(bf16[64,128,400]{1,2,0:T(8,128)(2,1)} %gather_fusion) | data formatting | bytes 13107200 | tf_op jit(solution)/shard_map/jit(_take)/gather | solution.py:133
  238.4 7.4 bitcast_select_fusion
  245.8 5.3 gather_fusion.5
  251.1 5.3 gather_fusion.4
  256.4 8.5 %gather_fusion.3 = bf16[1024,400]{1,0:T(8,128)(2,1)S(1)} fusion(bf16[8192,400]{1,0:T(8,128)(2,1)} %bitcast_select_fusion, s32[1024]{0:T(1024)S(1)} %fusion.19), kind=kCustom, calls=%fused_computation.2.clone | custom fusion | bytes 1642496 | tf_op jit(solution)/shard_map/while/body/eval_jaxpr/jit(_take)/gather | solution.py:20
  264.8 8.5 %gather_fusion.2 = bf16[1024,400]{1,0:T(8,128)(2,1)S(1)} fusion(bf16[8192,400]{1,0:T(8,128)(2,1)} %bitcast_select_fusion, s32[1024]{0:T(1024)S(1)} %fusion.18), kind=kCustom, calls=%fused_computation.clone | custom fusion | bytes 1642496 | tf_op jit(solution)/shard_map/while/body/eval_jaxpr/jit(_take)/gather | solution.py:19
  292.1 5.5 copy.68
  297.6 23.0 %scatter_custom_fusion = f32[8192,400]{1,0:T(8,128)} fusion(s32[2248]{0:T(1024)S(1)} %fusion.17, f32[2248,400]{1,0:T(8,128)} %copy.68, f32[]{:T(128)} %constant.55.clone.1), kind=kCustom, calls=%fused_computation.11 | custom fusion | flops 899200 | bytes 13107712 | tf_op jit(solution)/shard_map/while/body/eval_jaxpr/scatter-add | solution.py:104
  320.6 16.4 %copy.70 = f32[64,128,400]{1,2,0:T(8,128)} copy(f32[64,128,400]{2,1,0:T(8,128)} %bitcast.30) | data formatting | bytes 26214400 | tf_op jit(solution)/shard_map/reshape | solution.py:138
  337.0 5.5 broadcast_in_dim.87
  342.5 27.5 %scatter_fusion = f32[64,128,400]{1,2,0:T(8,128)} fusion(f32[64,128,400]{1,2,0:T(8,128)} %broadcast_in_dim.87, s32[64]{0:T(128)S(1)} %fusion.22, f32[64,128,400]{1,2,0:T(8,128)} %copy.70), kind=kCustom, calls=%fused_computation.7 | custom fusion | bytes 39321856 | tf_op jit(solution)/shard_map/scatter | solution.py:138
  369.9 8.1 %all-to-all-start.2 = ((f32[64,128,400]{1,2,0:T(8,128)}), f32[64,128,400]{1,2,0:T(8,128)}, u32[]{:S(2)}, u32[]{:S(2)}) async-start(f32[64,128,400]{1,2,0:T(8,128)} %scatter_fusion), calls=%async_computation.2 | async-start | bytes 26214400 | tf_op jit(solution)/shard_map/all_to_all | solution.py:139
  382.8 8.9 %scatter_custom_fusion.2 = f32[1300,400]{1,0:T(8,128)} fusion(s32[1024]{0:T(1024)S(1)} %get-tuple-element.61, f32[1024,400]{1,0:T(8,128)} %copy.72, f32[]{:T(128)} %constant.55.clone.1), kind=kCustom, calls=%fused_computation.19 | custom fusion | flops 409600 | bytes 2080512 | tf_op jit(solution)/shard_map/while/body/eval_jaxpr/scatter-add | solution.py:104
  391.6 331.7 %all-reduce.2.cloned.1.call-done = f32[1300,400]{1,0:T(8,128)} async-done(((f32[1300,400]{1,0:T(8,128)}), f32[1300,400]{1,0:T(8,128)}) %all-reduce.2.cloned.1.call-update) | async-done | bytes 2080016 | tf_op jit(solution)/shard_map/psum | solution.py:147
  726.5 15.8 %copy.71 = f32[64,128,400]{2,1,0:T(8,128)} copy(f32[64,128,400]{1,2,0:T(8,128)} %all-to-all-done.2) | data formatting | bytes 26214400 | tf_op jit(solution)/shard_map/all_to_all | solution.py:139
  742.3 15.5 %reshape.299 = f32[64,51200]{1,0:T(8,128)} reshape(f32[64,128,400]{2,1,0:T(8,128)} %copy.71) | data formatting | bytes 26214400 | tf_op jit(solution)/shard_map/reshape | solution.py:142
  757.8 7.3 fusion.14
  (80 shorter events, 50.6 us)
Async XLA Ops:
  9.3 19.7 %all-to-all-start = ((s32[64,1,1]{2,1,0:T(1,128)}), s32[64,1,1]{2,1,0:T(1,128)S(1)}, u32[]{:S(2)}, u32[]{:S(2)}) async-start(s32[64,1,1]{2,1,0:T(1,128)} %copy.60), calls=%async_computation | async-start | bytes 65536 | tf_op jit(solution)/shard_map/all_to_all | solution.py:125
  68.6 152.2 %all-to-all-start.1 = ((bf16[64,128,400]{1,2,0:T(8,128)(2,1)}), bf16[64,128,400]{1,2,0:T(8,128)(2,1)}, u32[]{:S(2)}, u32[]{:S(2)}) async-start(bf16[64,128,400]{1,2,0:T(8,128)(2,1)} %copy.62), calls=%async_computation.1 | async-start | bytes 13107200 | tf_op jit(solution)/shard_map/all_to_all | solution.py:132
  76.8 2.5 copy-start.7
  84.2 1.9 copy-start.5
  84.2 1.9 copy-start.6
  84.2 1.9 copy-start.8
  84.2 1.9 copy-start.9
  84.2 2.1 copy-start.10
  275.9 1.9 copy-start
  277.9 1.1 copy-start.2
  281.7 1.7 copy-start.1
  283.5 1.5 copy-start.3
  286.5 1.3 copy-start.4
  369.9 356.6 %all-to-all-start.2 = ((f32[64,128,400]{1,2,0:T(8,128)}), f32[64,128,400]{1,2,0:T(8,128)}, u32[]{:S(2)}, u32[]{:S(2)}) async-start(f32[64,128,400]{1,2,0:T(8,128)} %scatter_fusion), calls=%async_computation.2 | async-start | bytes 26214400 | tf_op jit(solution)/shard_map/all_to_all | solution.py:139
  378.1 345.3 %all-reduce.2.cloned.1.call-start = ((), (), s32[]{:S(2)}) async-start(), calls=%async_computation.3 | async-start | bytes 5341184 | tf_op jit(solution)/shard_map/psum | solution.py:147
Sparse Core Ops, SparseCore 0:
  391.8 331.5 all-reduce.1
where the time goes:
time: 783 us; the launch traced here: 775 us
  waiting for transfers between devices  470 us (60%)
  local copies, waits for them, and re-layouts  190 us (24%)
  other arithmetic  52.8 us (7%)
  starting transfers between devices  28.6 us (4%)
  matrix products  18.4 us (2%)
  between operations  14.7 us (2%)
    psum x1, waiting for transfers between devices, per_device(): relation_grad = lax.psum(rel_part, ('bucket', 'row'))  332 us
    all_to_all x1, waiting for transfers between devices, per_device(): lax.all_to_all(reply, 'bucket', split_axis=0, concat_axis=0, tiled=True)  133 us
    reshape x2, local copies, waits for them, and re-layouts, per_device(): reply = reply.reshape(bucket_count, block_rows, width)  31.2 us
    scatter x1, local copies, waits for them, and re-layouts, per_device(): outgoing.at[owners].set(buffer_grad.reshape(touched, block_rows, width))  27.5 us
    scatter-add x1, other arithmetic, advance(): totals[0].at[row_ids].add(row_vals)  23 us
    gather x2, local copies, waits for them, and re-layouts, per_device(): jnp.take(fetched, owners, axis=0).reshape(touched * block_rows, width)  17.7 us
    reshape x1, local copies, waits for them, and re-layouts, per_device(): buffer_grad.reshape(touched, block_rows, width)  16.4 us
    all_to_all x1, local copies, waits for them, and re-layouts, per_device(): lax.all_to_all(outgoing, 'bucket', split_axis=0, concat_axis=0, tiled=True)  15.8 us
  transfers between devices with their start and end apart: 4, of which 3 were waited for; matrix products, arithmetic and copies ran while one was open for 4% of the time, Pallas kernels for 0%

commit v1 on v0

--- a/solution.py
+++ b/solution.py
@@ -1,9 +1,660 @@
+import functools
+
 import jax
 import jax.numpy as jnp
 from jax import lax
+from jax.experimental import pallas as pl
+from jax.experimental.pallas import tpu as pltpu
 from jax.sharding import PartitionSpec as P
 
 BLOCK = 128
+WIDTH = 400
+EDGES = 1024
+NEG = 100
+REL = 1300
+REL_PAD = 1536
+ALL = 2 * EDGES + 2 * BLOCK
+XS, ZS, CS, YS = 4, 8, 2, 4
+XG = XS * CS
+TILES = 3
+CAP = TILES * BLOCK
+DIST = (0, 1, 7, 2, 6, 3, 5, 4)
+FIRST_OF_TILE = (3, 6, 8)
+TILES_OF = (0, 0, 0, 1, 1, 1, 2, 2)
+HALF = 208
+HALF_START = 192
+BF = jnp.bfloat16
+F32 = jnp.float32
+I32 = jnp.int32
+NT = (((1,), (1,)), ((), ()))
+TN = (((0,), (0,)), ((), ()))
+MIB = 1024 * 1024
+
+
+def mm(a, b, dims=(((1,), (0,)), ((), ()))):
+    return lax.dot_general(a, b, dims, preferred_element_type=F32)
+
+
+def iota(shape, dim):
+    return lax.broadcasted_iota(I32, shape, dim)
+
+
+def hot(mask):
+    return jnp.where(mask, 1.0, 0.0).astype(BF)
+
+
+def place():
+    b = lax.axis_index("bucket")
+    return b // (ZS * CS), (b // CS) % ZS, b % CS, lax.axis_index("row")
+
+
+def bucket_of(x, z, c):
+    return (x * ZS + z) * CS + c
+
+
+def x_peer(x, z, c, k):
+    s = lax.rem(x * CS + c + k, XG)
+    return s, {"bucket": bucket_of(s // CS, z, s % CS)}
+
+
+def z_peer(x, z, c, k):
+    other = lax.rem(z + k, ZS)
+    return other, {"bucket": bucket_of(x, other, c)}
+
+
+def greet(peers):
+    barrier = pltpu.get_barrier_semaphore()
+    for peer in peers:
+        pl.semaphore_signal(barrier, inc=1, device_id=peer, device_id_type=pl.DeviceIdType.MESH)
+    pl.semaphore_wait(barrier, len(peers))
+
+
+def remote(src, dst, send, recv, peer):
+    return pltpu.make_async_remote_copy(
+        src_ref=src, dst_ref=dst, send_sem=send, recv_sem=recv,
+        device_id=peer, device_id_type=pl.DeviceIdType.MESH,
+    )
+
+
+def plan_rows(ids, owners, blocks, z):
+    slot = lax.shift_right_arithmetic(ids, 7)
+    row = jnp.bitwise_and(ids, 127)
+    slot_hot = hot(iota((64, ALL), 0) == slot)
+    row_is = iota((BLOCK, ALL), 0) == row
+    row_hot = hot(row_is)
+    count = mm(slot_hot, row_hot, NT)
+    wanted_slot = hot(count > 0.5)
+    j = iota((64, 64), 0)
+    s, q = j // 8, j % 8
+    dist = jnp.where(q % 2 == 1, (q + 1) // 2, (8 - q // 2) % 8)
+    target = bucket_of(s // CS, (z + dist) % ZS, s % CS)
+    perm_is = owners == target
+    perm = hot(perm_is)
+    wanted = mm(perm, wanted_slot)
+    block = jnp.sum(jnp.where(perm_is, blocks, 0), axis=1, keepdims=True)
+    wanted_low = wanted.astype(BF)
+    before = mm(wanted_low, hot(iota((BLOCK, BLOCK), 0) < iota((BLOCK, BLOCK), 1)))
+    number = mm(wanted_low, jnp.ones((BLOCK, BLOCK), BF)).astype(BF)
+    jj = iota((64, 64), 1)
+    same = s == jj // 8
+    qq = jj % 8
+
+    def tile_of(position):
+        return jnp.where(position < 3, 0, jnp.where(position < 6, 1, 2))
+
+    lead = mm(hot(same & (tile_of(q) == tile_of(qq)) & (qq < q)), number)
+    sums = [mm(hot(same & (tile_of(qq) == t)), number) for t in range(TILES)]
+    start1 = jnp.maximum(float(BLOCK), sums[0])
+    start2 = jnp.maximum(float(2 * BLOCK), start1 + sums[1])
+    end = start2 + sums[2]
+    q_wide = iota((64, BLOCK), 0) % 8
+    start = jnp.where(q_wide < 3, 0.0, jnp.where(q_wide < 6, start1, start2))
+    rank = (start + lead + before).astype(I32)
+    codes = jnp.where(wanted > 0.5, block * 1024 + rank, -1)
+    overflow = jnp.max(jnp.where(end > float(CAP), 1.0, 0.0))
+    position = (iota((64, BLOCK), 0) // 8) * CAP + rank
+    high = lax.shift_right_arithmetic(position, 7).astype(F32).astype(BF)
+    low = jnp.bitwise_and(position, 127).astype(F32).astype(BF)
+    high_slot = mm(perm, high, TN).astype(BF)
+    low_slot = mm(perm, low, TN).astype(BF)
+    high_ids = mm(high_slot, slot_hot, TN)
+    low_ids = mm(low_slot, slot_hot, TN)
+    value = jnp.sum(jnp.where(row_is, high_ids * 128.0 + low_ids, 0.0), axis=0, keepdims=True)
+    places = jnp.where(slot >= 0, value.astype(I32), -1)
+    return codes, places, overflow
+
+
+def twice(row):
+    return jnp.concatenate([row, row], axis=1)
+
+
+def fetch_kernel(
+    ent_ref, ids_ref, owner_ref, block_ref, rows_ref, place_ref, code_ref, flag_ref,
+    tables, codes_mine, codes_in, stage, landed, total,
+    ring_send, ring_recv, ask_send, ask_recv, tile_send, tile_recv,
+):
+    x, z, c, _ = place()
+    me = x * CS + c
+    _, right = z_peer(x, z, c, 1)
+    _, left = z_peer(x, z, c, ZS - 1)
+    peers = [x_peer(x, z, c, k) for k in range(XG)]
+    for half in range(2):
+        tables[0, half] = ent_ref[:, half * 256 : (half + 1) * 256].astype(BF)
+    greet([right, left] + [peer for _, peer in peers[1:]])
+
+    def ring(way, step, half):
+        if way == 0:
+            src, dst = (-step) % ZS, (-step - 1) % ZS
+        else:
+            src, dst = step, step + 1
+        return remote(
+            tables.at[src, half], tables.at[dst, half],
+            ring_send.at[way, step, half], ring_recv.at[way, step, half],
+            right if way == 0 else left,
+        )
+
+    def legs(step):
+        if step < 3:
+            return [(0, 0), (1, 0), (0, 1), (1, 1)]
+        return [(0, 1), (1, 0)]
+
+    for way, half in legs(0):
+        ring(way, 0, half).start()
+
+    def forward(step):
+        for way, half in legs(step):
+            ring(way, step, half).wait_recv()
+            if step < 3 and (way, half) in legs(step + 1):
+                ring(way, step + 1, half).start()
+
+    codes, places, overflow = plan_rows(ids_ref[...], owner_ref[...], block_ref[...], z)
+    codes_mine[...] = codes.reshape(XG, 8, BLOCK)
+    place_ref[...] = places
+    flag_ref[...] = jnp.zeros((8, BLOCK), F32) + overflow
+
+    def ask(k):
+        s, peer = peers[k]
+        return remote(codes_mine.at[s], codes_in.at[me], ask_send.at[k], ask_recv.at[k], peer)
+
+    for k in range(1, XG):
+        ask(k).start()
+    codes_in[me] = codes_mine[me]
+
+    def tile(t, k):
+        s, peer = peers[k]
+        return remote(
+            stage.at[t, k], landed.at[t, me], tile_send.at[t, k], tile_recv.at[t, k], peer
+        )
+
+    def select(t):
+        parts = [(q, half) for q in range(FIRST_OF_TILE[t]) for half in range(2)]
+        lhs = jnp.concatenate([tables[DIST[q], half] for q, half in parts], axis=1)
+        key = (iota((BLOCK, 256), 1) // BLOCK) * 1024 + iota((BLOCK, 256), 0) + t * BLOCK
+        for pair in range(XG // 2):
+            both = (2 * pair + 1, (2 * pair + 2) % XG)
+            chosen = []
+            for k in both:
+                code = codes_in[peers[k][0]]
+                chosen.append(
+                    jnp.concatenate(
+                        [hot(twice(code[q : q + 1]) == key + 2048 * half) for q, half in parts],
+                        axis=1,
+                    )
+                )
+            rows = mm(lhs, jnp.concatenate(chosen, axis=0), NT).astype(BF)
+            for i, k in enumerate(both):
+                part = rows[:, i * BLOCK : (i + 1) * BLOCK]
+                if k == 0:
+                    landed[t, me] = part
+                else:
+                    stage[t, k] = part
+                    tile(t, k).start()
+
+    def gather(t):
+        for k in range(1, XG):
+            s = lax.rem(me + XG - k, XG)
+            _, peer = peers[k]
+            remote(
+                stage.at[t, k], landed.at[t, s], tile_send.at[t, k], tile_recv.at[t, k], peer
+            ).wait_recv()
+        key = iota((XG * BLOCK, 256), 0)
+        key = (key // BLOCK) * CAP + key % BLOCK + t * BLOCK
+
+        def chunk(i, carry):
+            lanes = pl.ds(pl.multiple_of(i * 256, 256), 256)
+            lhs = jnp.concatenate([landed[t, s] for s in range(XG)], axis=1)
+            rows = mm(lhs, hot(key == place_ref[:, lanes]))
+            if t == 0:
+                total[:, lanes] = rows
+            elif t < TILES - 1:
+                total[:, lanes] += rows
+            else:
+                rows_ref[:, lanes] = (total[:, lanes] + rows).astype(BF)
+            return carry
+
+        lax.fori_loop(0, ALL // 256, chunk, 0)
+
+    forward(0)
+    for k in range(1, XG):
+        s = lax.rem(me + XG - k, XG)
+        remote(
+            codes_mine.at[s], codes_in.at[s], ask_send.at[k], ask_recv.at[k], peers[k][1]
+        ).wait_recv()
+    code_ref[...] = codes_in[...]
+    select(0)
+    forward(1)
+    gather(0)
+    forward(2)
+    select(1)
+    forward(3)
+    select(2)
+    gather(1)
+    gather(2)
+    for step in range(4):
+        for way, half in legs(step):
+            ring(way, step, half).wait_send()
+    for k in range(1, XG):
+        ask(k).wait_send()
+        for t in range(TILES):
+            tile(t, k).wait_send()
+
+
+def vmem():
+    return pl.BlockSpec(memory_space=pltpu.VMEM)
+
+
+def fetch(ent, ids, owners, blocks):
+    dma = pltpu.SemaphoreType.DMA
+    return pl.pallas_call(
+        fetch_kernel,
+        out_shape=(
+            jax.ShapeDtypeStruct((WIDTH, ALL), BF),
+            jax.ShapeDtypeStruct((1, ALL), I32),
+            jax.ShapeDtypeStruct((XG, 8, BLOCK), I32),
+            jax.ShapeDtypeStruct((8, BLOCK), F32),
+        ),
+        in_specs=[vmem()] * 4,
+        out_specs=[vmem()] * 4,
+        scratch_shapes=[
+            pltpu.VMEM((ZS, 2, WIDTH, 256), BF),
+            pltpu.VMEM((XG, 8, BLOCK), I32),
+            pltpu.VMEM((XG, 8, BLOCK), I32),
+            pltpu.VMEM((TILES, XG, WIDTH, BLOCK), BF),
+            pltpu.VMEM((TILES, XG, WIDTH, BLOCK), BF),
+            pltpu.VMEM((WIDTH, ALL), F32),
+            dma((2, 4, 2)), dma((2, 4, 2)),
+            dma((XG,)), dma((XG,)),
+            dma((TILES, XG)), dma((TILES, XG)),
+        ],
+        compiler_params=pltpu.CompilerParams(
+            collective_id=0, has_side_effects=True, vmem_limit_bytes=56 * MIB
+        ),
+        name="fetch",
+    )(ent, ids, owners, blocks)
+
+
+def side(positive, scores, valid):
+    largest = jnp.maximum(
+        positive, jnp.max(jnp.where(valid, scores, -3e38), axis=0, keepdims=True)
+    )
+    own = jnp.exp(positive - largest)
+    others = jnp.where(valid, jnp.exp(scores - largest), 0.0)
+    total = own + jnp.sum(others, axis=0, keepdims=True)
+    return own / total - 1.0, others / total
+
+
+def edge_kernel(rows_ref, rel_ref, rel_ids_ref, flag_ref, grads_ref, relg_ref, hot_rel, high, low, edge_rel, neg_sum):
+    mid = WIDTH // 2
+    high[...] = jnp.zeros_like(high)
+    low[...] = jnp.zeros_like(low)
+    rel = rel_ref[...]
+    rel_high = rel.astype(BF)
+    high[:, 0:REL] = rel_high
+    low[:, 0:REL] = (rel - rel_high.astype(F32)).astype(BF)
+    neg_sum[...] = jnp.zeros_like(neg_sum)
+    step = 256
+
+    def chunk(i, carry):
+        lanes = pl.ds(pl.multiple_of(i * step, step), step)
+        tail_lanes = pl.ds(pl.multiple_of(EDGES + i * step, step), step)
+        which = hot(iota((REL_PAD, step), 0) == rel_ids_ref[:, lanes])
+        hot_rel[:, lanes] = which
+        relation = mm(high[...], which) + mm(low[...], which)
+        a, b = relation[:mid], relation[mid:]
+        head = rows_ref[:, lanes].astype(F32)
+        tail = rows_ref[:, tail_lanes].astype(F32)
+        hr, hi = head[:mid], head[mid:]
+        tr, ti = tail[:mid], tail[mid:]
+        query = jnp.concatenate([hr * a - hi * b, hr * b + hi * a], axis=0)
+        probe = jnp.concatenate([a * tr + b * ti, a * ti - b * tr], axis=0)
+        positive = jnp.sum(query * tail, axis=0, keepdims=True)
+        query_low, probe_low = query.astype(BF), probe.astype(BF)
+        tail_neg = rows_ref[:, 2 * EDGES : 2 * EDGES + BLOCK]
+        head_neg = rows_ref[:, 2 * EDGES + BLOCK : 2 * EDGES + 2 * BLOCK]
+        valid = iota((BLOCK, step), 0) < NEG
+        tail_coef, tail_weights = side(positive, mm(tail_neg, query_low, TN), valid)
+        head_coef, head_weights = side(positive, mm(head_neg, probe_low, TN), valid)
+        tail_low, head_low = tail_weights.astype(BF), head_weights.astype(BF)
+        both = tail_coef + head_coef
+        qg = both * tail + mm(tail_neg, tail_low)
+        pg = mm(head_neg, head_low)
+        neg_sum[0] += mm(query_low, tail_low, NT)
+        neg_sum[1] += mm(probe_low, head_low, NT)
+        qr, qi = qg[:mid], qg[mid:]
+        pr, pi = pg[:mid], pg[mid:]
+        grads_ref[:, lanes] = jnp.concatenate(
+            [qr * a + qi * b, qi * a - qr * b], axis=0
+        ).astype(BF)
+        grads_ref[:, tail_lanes] = (
+            both * query + jnp.concatenate([pr * a - pi * b, pr * b + pi * a], axis=0)
+        ).astype(BF)
+        edge_rel[:, lanes] = jnp.concatenate(
+            [
+                qr * hr + qi * hi + pr * tr + pi * ti,
+                qi * hr - qr * hi + pr * ti - pi * tr,
+            ],
+            axis=0,
+        ).astype(BF)
+        return carry
+
+    lax.fori_loop(0, EDGES // step, chunk, 0)
+    grads_ref[:, 2 * EDGES : 2 * EDGES + BLOCK] = neg_sum[0].astype(BF)
+    grads_ref[:, 2 * EDGES + BLOCK : 2 * EDGES + 2 * BLOCK] = neg_sum[1].astype(BF)
+
+    def scatter(i, carry):
+        lanes = pl.ds(pl.multiple_of(i * 256, 256), 256)
+        relg_ref[:, lanes] = mm(edge_rel[...], hot_rel[lanes, :], NT)
+        return carry
+
+    lax.fori_loop(0, REL_PAD // 256, scatter, 0)
+    spare = iota((WIDTH, BLOCK), 1) + (REL_PAD - BLOCK) >= REL
+    relg_ref[:, REL_PAD - BLOCK :] = jnp.where(
+        spare, flag_ref[0:1, :], relg_ref[:, REL_PAD - BLOCK :]
+    )
+
+
+def edge_grads(rows, rel, rel_ids, flag):
+    return pl.pallas_call(
+        edge_kernel,
+        out_shape=(
+            jax.ShapeDtypeStruct((WIDTH, ALL), BF),
+            jax.ShapeDtypeStruct((WIDTH, REL_PAD), F32),
+        ),
+        in_specs=[vmem()] * 4,
+        out_specs=[vmem()] * 2,
+        scratch_shapes=[
+            pltpu.VMEM((REL_PAD, EDGES), BF),
+            pltpu.VMEM((WIDTH, REL_PAD), BF),
+            pltpu.VMEM((WIDTH, REL_PAD), BF),
+            pltpu.VMEM((WIDTH, EDGES), BF),
+            pltpu.VMEM((2, WIDTH, BLOCK), F32),
+        ],
+        compiler_params=pltpu.CompilerParams(vmem_limit_bytes=56 * MIB),
+        name="edges",
+    )(rows, rel, rel_ids, flag)
+
+
+def give_kernel(
+    grads_ref, place_ref, code_ref, relg_ref, ent_ref, rel_ref, flag_ref,
+    stage, landed, ring_out, ring_in,
+    core_out, core_in, y_out, y_in, z_out, z_in, x_out, x_in, zg_out, zg_in, yg_out, yg_in, cg_in,
+    sum_core, sum_y,
+    tile_send, tile_recv, ring_send, ring_recv,
+    core_send, core_recv, y_send, y_recv, z_send, z_recv, x_send, x_recv,
+    zg_send, zg_recv, yg_send, yg_recv, cg_send, cg_recv,
+):
+    x, z, c, y = place()
+    me = x * CS + c
+    z_peers = [z_peer(x, z, c, k) for k in range(ZS)]
+    x_peers = [x_peer(x, z, c, k) for k in range(XG)]
+    y_peers = [(lax.rem(y + k, YS), {"row": lax.rem(y + k, YS)}) for k in range(YS)]
+    same_core = [
+        (lax.rem(x + k, XS), {"bucket": bucket_of(lax.rem(x + k, XS), z, c)}) for k in range(XS)
+    ]
+    mate = {"bucket": bucket_of(x, z, 1 - c)}
+    right, left = z_peers[1][1], z_peers[ZS - 1][1]
+    greet([p for _, p in z_peers[1:]] + [p for _, p in x_peers[1:]] + [p for _, p in y_peers[1:]])
+
+    def core_copy():
+        return remote(core_out, core_in, core_send, core_recv, mate)
+
+    def rel_core():
+        core_out[...] = relg_ref[pl.ds(pl.multiple_of((1 - c) * HALF_START, 16), HALF), :].astype(BF)
+        core_copy().start()
+
+    def y_copy(k):
+        return remote(y_out.at[k], y_in.at[k], y_send.at[k], y_recv.at[k], y_peers[k][1])
+
+    def rel_y():
+        core_copy().wait_recv()
+        mine = pl.ds(pl.multiple_of(c * HALF_START, 16), HALF)
+        sum_core[...] = relg_ref[mine, :] + core_in[...].astype(F32)
+        for k in range(1, YS):
+            other = y_peers[k][0]
+            y_out[k] = sum_core[:, pl.ds(pl.multiple_of(other * 384, 128), 384)].astype(BF)
+            y_copy(k).start()
+
+    def z_copy(k):
+        return remote(z_out.at[k], z_in.at[k], z_send.at[k], z_recv.at[k], z_peers[k][1])
+
+    def rel_z():
+        for k in range(1, YS):
+            y_copy(k).wait_recv()
+        summed = sum_core[:, pl.ds(pl.multiple_of(y * 384, 128), 384)]
+        for k in range(1, YS):
+            summed = summed + y_in[k].astype(F32)
+        sum_y[...] = jnp.zeros_like(sum_y)
+        sum_y[0:HALF, :] = summed
+        for k in range(1, ZS):
+            other = z_peers[k][0]
+            z_out[k] = sum_y[pl.ds(pl.multiple_of(other * 32, 32), 32), :].astype(BF)
+            z_copy(k).start()
+
+    def x_copy(k):
+        return remote(x_out, x_in.at[x], x_send.at[k], x_recv.at[k], same_core[k][1])
+
+    def rel_x():
+        for k in range(1, ZS):
+            z_copy(k).wait_recv()
+        summed = sum_y[pl.ds(pl.multiple_of(z * 32, 32), 32), :]
+        for k in range(1, ZS):
+            summed = summed + z_in[k].astype(F32)
+        x_out[...] = summed
+        x_in[x] = summed
+        for k in range(1, XS):
+            x_copy(k).start()
+
+    def zg_copy(k):
+        return remote(zg_out, zg_in.at[z], zg_send.at[k], zg_recv.at[k], z_peers[k][1])
+
+    def rel_zg():
+        for k in range(1, XS):
+            s = lax.rem(x + XS - k, XS)
+            remote(x_out, x_in.at[s], x_send.at[k], x_recv.at[k], same_core[k][1]).wait_recv()
+        summed = ((x_in[0] + x_in[1]) + (x_in[2] + x_in[3])).astype(BF)
+        zg_out[...] = summed
+        zg_in[z] = summed
+        for k in range(1, ZS):
+            zg_copy(k).start()
+
+    def yg_copy(k):
+        return remote(yg_out, yg_in.at[y], yg_send.at[k], yg_recv.at[k], y_peers[k][1])
+
+    def rel_yg():
+        for k in range(1, ZS):
+            s = lax.rem(z + ZS - k, ZS)
+            remote(zg_out, zg_in.at[s], zg_send.at[k], zg_recv.at[k], z_peers[k][1]).wait_recv()
+        whole = jnp.concatenate([zg_in[i] for i in range(ZS)], axis=0)[0:HALF]
+        yg_out[...] = whole
+        yg_in[y] = whole
+        for k in range(1, YS):
+            yg_copy(k).start()
+
+    def cg_copy():
+        return remote(yg_in, cg_in, cg_send, cg_recv, mate)
+
+    def rel_cg():
+        for k in range(1, YS):
+            s = lax.rem(y + YS - k, YS)
+            remote(yg_out, yg_in.at[s], yg_send.at[k], yg_recv.at[k], y_peers[k][1]).wait_recv()
+        cg_copy().start()
+
+    def rel_end():
+        cg_copy().wait_recv()
+        for i in range(YS):
+            mine, other = yg_in[i].astype(F32), cg_in[i].astype(F32)
+            first = jnp.where(c == 0, mine, other)
+            second = jnp.where(c == 0, other, mine)
+            whole = jnp.concatenate([first, second[HALF - HALF_START :]], axis=0)
+            if i < YS - 1:
+                rel_ref[:, i * 384 : (i + 1) * 384] = whole
+            else:
+                rel_ref[:, i * 384 : REL] = whole[:, : REL - i * 384]
+                flag_ref[...] = whole[0:8, 256:384]
+
+    def tile(t, k):
+        return remote(
+            stage.at[t, k], landed.at[t, me], tile_send.at[t, k], tile_recv.at[t, k], x_peers[k][1]
+        )
+
+    def scatter(t):
+        for pair in range(XG // 2):
+            both = (2 * pair + 1, (2 * pair + 2) % XG)
+            row = iota((BLOCK, ALL), 0) + t * BLOCK
+            which = jnp.concatenate(
+                [hot(row + x_peers[k][0] * CAP == place_ref[...]) for k in both], axis=0
+            )
+            rows = mm(grads_ref[...], which, NT).astype(BF)
+            for i, k in enumerate(both):
+                part = rows[:, i * BLOCK : (i + 1) * BLOCK]
+                if k == 0:
+                    landed[t, me] = part
+                else:
+                    stage[t, k] = part
+                    tile(t, k).start()
+
+    def arrive(t):
+        for k in range(1, XG):
+            s = lax.rem(me + XG - k, XG)
+            remote(
+                stage.at[t, k], landed.at[t, s], tile_send.at[t, k], tile_recv.at[t, k],
+                x_peers[k][1],
+            ).wait_recv()
+
+    def partial(dist, half):
+        q = DIST.index(dist)
+        parts = [(t, s) for t in range(TILES_OF[q], TILES) for s in range(XG)]
+        lhs = jnp.concatenate([landed[t, s] for t, s in parts], axis=1)
+        key = (iota((BLOCK, 256), 1) // BLOCK + 2 * half) * 1024 + iota((BLOCK, 256), 0)
+        which = jnp.concatenate(
+            [hot(twice(code_ref[s, q : q + 1]) == key + t * BLOCK) for t, s in parts], axis=0
+        )
+        return mm(lhs, which)
+
+    def ring(way, step, half):
+        return remote(
+            ring_out.at[way, step, half], ring_in.at[way, step, half],
+            ring_send.at[way, step, half], ring_recv.at[way, step, half],
+            right if way == 0 else left,
+        )
+
+    def has(way, step, half):
+        return 0 < step or half == 1 - way
+
+    def push(step, way):
+        dist = 4 - step if way == 0 else (4 + step) % ZS
+        order = (0, 1) if way == 0 else (1, 0)
+        for half in order:
+            if not has(way, step, half):
+                continue
+            value = partial(dist, half)
+            if step > 0 and has(way, step - 1, half):
+                ring(way, step - 1, half).wait_recv()
+                value = value + ring_in[way, step - 1, half].astype(F32)
+            ring_out[way, step, half] = value.astype(BF)
+            ring(way, step, half).start()
+
+    rel_core()
+    scatter(2)
+    rel_y()
+    scatter(1)
+    scatter(0)
+    arrive(2)
+    push(0, 0)
+    push(0, 1)
+    push(1, 1)
+    rel_z()
+    arrive(1)
+    push(1, 0)
+    rel_x()
+    push(2, 1)
+    push(2, 0)
+    rel_zg()
+    arrive(0)
+    push(3, 1)
+    push(3, 0)
+    rel_yg()
+    own = [partial(0, half) for half in range(2)]
+    rel_cg()
+    for half in range(2):
+        ring(0, 3, half).wait_recv()
+        ring(1, 3, half).wait_recv()
+        ent_ref[:, half * 256 : (half + 1) * 256] = (
+            own[half] + ring_in[0, 3, half].astype(F32) + ring_in[1, 3, half].astype(F32)
+        )
+    rel_end()
+
+    core_copy().wait_send()
+    cg_copy().wait_send()
+    for k in range(1, YS):
+        y_copy(k).wait_send()
+        yg_copy(k).wait_send()
+    for k in range(1, ZS):
+        z_copy(k).wait_send()
+        zg_copy(k).wait_send()
+    for k in range(1, XS):
+        x_copy(k).wait_send()
+    for k in range(1, XG):
+        for t in range(TILES):
+            tile(t, k).wait_send()
+    for way in range(2):
+        for step in range(4):
+            for half in range(2):
+                if has(way, step, half):
+                    ring(way, step, half).wait_send()
+
+
+def give(grads, places, codes, relg):
+    dma = pltpu.SemaphoreType.DMA
+    v = pltpu.VMEM
+    return pl.pallas_call(
+        give_kernel,
+        out_shape=(
+            jax.ShapeDtypeStruct((WIDTH, 512), F32),
+            jax.ShapeDtypeStruct((WIDTH, REL), F32),
+            jax.ShapeDtypeStruct((8, BLOCK), F32),
+        ),
+        in_specs=[vmem()] * 4,
+        out_specs=[vmem()] * 3,
+        scratch_shapes=[
+            v((TILES, XG, WIDTH, BLOCK), BF), v((TILES, XG, WIDTH, BLOCK), BF),
+            v((2, 4, 2, WIDTH, 256), BF), v((2, 4, 2, WIDTH, 256), BF),
+            v((HALF, REL_PAD), BF), v((HALF, REL_PAD), BF),
+            v((YS, HALF, 384), BF), v((YS, HALF, 384), BF),
+            v((ZS, 32, 384), BF), v((ZS, 32, 384), BF),
+            v((32, 384), F32), v((XS, 32, 384), F32),
+            v((32, 384), BF), v((ZS, 32, 384), BF),
+            v((HALF, 384), BF), v((YS, HALF, 384), BF), v((YS, HALF, 384), BF),
+            v((HALF, REL_PAD), F32), v((256, 384), F32),
+            dma((TILES, XG)), dma((TILES, XG)), dma((2, 4, 2)), dma((2, 4, 2)),
+            dma, dma, dma((YS,)), dma((YS,)), dma((ZS,)), dma((ZS,)), dma((XS,)), dma((XS,)),
+            dma((ZS,)), dma((ZS,)), dma((YS,)), dma((YS,)), dma, dma,
+        ],
+        compiler_params=pltpu.CompilerParams(
+            collective_id=1, has_side_effects=True, vmem_limit_bytes=56 * MIB
+        ),
+        name="give",
+    )(grads, places, codes, relg)
 
 
 def side_weights(positive, scores):
@@ -109,7 +760,7 @@
     return totals
 
 
-def per_device(
+def dense_step(
     entities, relations, touch_owner, touch_block, head_ids, rel_ids, tail_ids, neg_tail, neg_head
 ):
     bucket_count = lax.axis_size("bucket")
@@ -146,6 +797,24 @@
     entity_grad = entity_grad.reshape(owned * block_rows, width)
     relation_grad = lax.psum(rel_part, ("bucket", "row"))
     return (entity_grad, relation_grad)
+
+
+def per_device(
+    entities, relations, touch_owner, touch_block, head_ids, rel_ids, tail_ids, neg_tail, neg_head
+):
+    spare = jnp.full((BLOCK - NEG,), -1, I32)
+    ids = jnp.concatenate([head_ids, tail_ids, neg_tail[0], spare, neg_head[0], spare])[None, :]
+    rows, places, codes, flag = fetch(entities.T, ids, touch_owner, touch_block)
+    grads, relg = edge_grads(rows, relations.T, rel_ids[None, :], flag)
+    ent, rel, over = give(grads, places, codes, relg)
+    return lax.cond(
+        over[0, 0] > 0.5,
+        lambda: dense_step(
+            entities, relations, touch_owner, touch_block, head_ids, rel_ids, tail_ids,
+            neg_tail, neg_head,
+        ),
+        lambda: (ent.T, rel.T),
+    )
 
 
 def solution(mesh):

time: 783 us -> 182 us (0.23)
  waiting for transfers between devices: 470 us -> 0 us
  local copies, waits for them, and re-layouts: 190 us -> 7.93 us
  Pallas kernels: 0 us -> 155 us
  other arithmetic: 52.8 us -> 0 us
  starting transfers between devices: 28.6 us -> 0 us
  matrix products: 18.4 us -> 0 us
    psum x1 -> x0, waiting for transfers between devices: 332 us -> none  [per_device(): relation_grad = lax.psum(rel_part, ('bucket', 'row'))]
    pallas_call x0 -> x3, Pallas kernels: none -> 155 us  [the longest x1 77.7 us: give(): pl.pallas_call(give_kernel, out_shape=(jax.ShapeDtypeStruct((WIDTH, 512),...]
    all_to_all x3 -> x0, waiting for transfers between devices: 138 us -> none  [the longest x1 133 us: per_device(): lax.all_to_all(reply, 'bucket', split_axis=0, concat_axis=0, tiled=True)]
    reshape x6 -> x0, local copies, waits for them, and re-layouts: 65.2 us -> none  [the longest x2 31.2 us: per_device(): reply = reply.reshape(bucket_count, block_rows, width)]
    gather x10 -> x0, local copies, waits for them, and re-layouts: 54.5 us -> none  [the longest x2 17.7 us: per_device(): jnp.take(fetched, owners, axis=0).reshape(touched * block_rows, width)]
    scatter-add x2 -> x0, other arithmetic: 31.8 us -> none  [the longest x1 23 us: advance(): totals[0].at[row_ids].add(row_vals)]
    all_to_all x3 -> x0, starting transfers between devices: 28.5 us -> none  [the longest x1 12.2 us: per_device(): lax.all_to_all(request, 'bucket', split_axis=0, concat_axis=0, tiled=True)]
    scatter x1 -> x0, local copies, waits for them, and re-layouts: 27.5 us -> none  [per_device(): outgoing.at[owners].set(buffer_grad.reshape(touched, block_rows, width))]
  transfers between devices with their start and end apart: 4 -> 0, of which waited for: 3 -> 0; matrix products, arithmetic and copies ran while one was open for 4% -> 0% of each run, Pallas kernels for 0% -> 0%
where the time goes in v1:
time: 182 us; the launch traced here: 179 us
  Pallas kernels  155 us (85%)
  between operations  15.1 us (8%)
  local copies, waits for them, and re-layouts  7.93 us (4%)
    pallas_call x1, Pallas kernels, give(): pl.pallas_call(give_kernel, out_shape=(jax.ShapeDtypeStruct((WIDTH, 512),...  77.7 us
    pallas_call x1, Pallas kernels, fetch(): pl.pallas_call(fetch_kernel, out_shape=(jax.ShapeDtypeStruct((WIDTH, ALL)...  62.5 us
    pallas_call x1, Pallas kernels, edge_grads(): pl.pallas_call(edge_kernel, out_shape=(jax.ShapeDtypeStruct((WIDTH, ALL),...  14.8 us
    unnamed x18, local copies, waits for them, and re-layouts  5.34 us

profile of v1, /device:TPU:6, one launch (start us, length us, event | category | flops | bytes accessed | tf_op | source)
XLA Modules:
  0.0 179.1 jit_solution(1437664348757154133)
XLA Ops:
  7.2 0.8 concatenate.59
  8.0 0.6 broadcast_in_dim.82.ids_ref
  8.6 62.5 %fetch.1 = (bf16[400,2304]{1,0:T(8,128)(2,1)}, s32[1,2304]{1,0:T(1,128)}, s32[8,8,128]{2,1,0:T(8,128)}, f32[8,128]{1,0:T(8,128)}) custom-call(f32[400,512]{1,0:T(8,128)} %bitcast.42, s32[1,2304]{1,0:T(1,128)} %broadcast_in_dim.82.ids_ref, s32[1,64]{1,0:T(1,128)} %owner_ref.1, s32[1,64]{1,0:T(1,128)} %block_ref.1), custom_call_target="tpu_custom_call" | custom-call | tf_op jit(solution)/shard_map/fetch/pallas_call | solution.py:268
  71.1 14.8 %edges.1 = (bf16[400,2304]{1,0:T(8,128)(2,1)}, f32[400,1536]{1,0:T(8,128)}) custom-call(bf16[400,2304]{1,0:T(8,128)(2,1)} %get-tuple-element.76.rows_ref, f32[400,1300]{1,0:T(8,128)} %bitcast.41, s32[1,1024]{1,0:T(1,128)} %bitcast.47, f32[8,128]{1,0:T(8,128)} %get-tuple-element.77.flag_ref), custom_call_target="tpu_custom_call" | custom-call | tf_op jit(solution)/shard_map/edges/pallas_call | solution.py:377
  85.8 77.7 %give.1 = (f32[400,512]{1,0:T(8,128)}, f32[400,1300]{1,0:T(8,128)}, f32[8,128]{1,0:T(8,128)}) custom-call(bf16[400,2304]{1,0:T(8,128)(2,1)} %get-tuple-element.78.grads_ref, s32[1,2304]{1,0:T(1,128)} %get-tuple-element.79.place_ref, s32[8,8,128]{2,1,0:T(8,128)} %get-tuple-element.80.code_ref, f32[400,1536]{1,0:T(8,128)} %get-tuple-element.81.relg_ref), custom_call_target="tpu_custom_call" | custom-call | tf_op jit(solution)/shard_map/give/pallas_call | solution.py:630
  163.6 1.2 slice.43
  165.4 2.1 %copy.107 = f32[400,512]{1,0:T(8,128)} copy(f32[400,512]{1,0:T(8,128)} %get-tuple-element.192) | data formatting | bytes 1638400
  167.5 0.0 copy-start.6
  167.5 0.0 copy-start.7
  167.5 0.0 copy-start.8
  167.5 0.0 copy-start.9
  167.5 0.0 copy-start.10
  167.5 0.0 copy-start.11
  167.5 0.0 copy-start.12
  167.6 3.2 %copy.108 = f32[400,1300]{1,0:T(8,128)} copy(f32[400,1300]{1,0:T(8,128)} %get-tuple-element.193) | data formatting | bytes 4160000
  170.8 0.0 copy-done.4
  170.8 0.0 copy-done.6
  170.8 0.0 copy-done.7
  170.8 0.0 copy-done.8
  170.8 0.0 copy-done.9
  170.8 0.0 copy-done.10
  170.8 0.0 copy-done.11
  170.8 0.0 copy-done.12
  170.8 1.1 conditional.1
  (2 shorter events, 0.0 us)
Async XLA Ops:
  167.5 3.3 %copy-start.4 = (f32[512,400]{0,1:T(8,128)S(1)}, f32[512,400]{0,1:T(8,128)}, u32[]{:S(2)}) copy-start(f32[512,400]{0,1:T(8,128)} %param.15) | copy-start | bytes 2457604
  167.5 3.3 %copy-start.6 = (s32[1024]{0:T(1024)S(1)}, s32[1024]{0:T(1024)}, u32[]{:S(2)}) copy-start(s32[1024]{0:T(1024)} %param.19) | copy-start | bytes 12292
  167.5 3.3 %copy-start.7 = (s32[1024]{0:T(1024)S(1)}, s32[1024]{0:T(1024)}, u32[]{:S(2)}) copy-start(s32[1024]{0:T(1024)} %param.21) | copy-start | bytes 12292
  167.5 3.3 %copy-start.8 = (s32[1024]{0:T(1024)S(1)}, s32[1024]{0:T(1024)}, u32[]{:S(2)}) copy-start(s32[1024]{0:T(1024)} %param.20) | copy-start | bytes 12292
  167.5 3.3 %copy-start.9 = (s32[1,100]{1,0:T(1,128)S(1)}, s32[1,100]{1,0:T(1,128)}, u32[]{:S(2)}) copy-start(s32[1,100]{1,0:T(1,128)} %param.22) | copy-start | bytes 1204
  167.5 3.3 %copy-start.10 = (s32[1,100]{1,0:T(1,128)S(1)}, s32[1,100]{1,0:T(1,128)}, u32[]{:S(2)}) copy-start(s32[1,100]{1,0:T(1,128)} %param.23) | copy-start | bytes 1204
  167.5 3.3 %copy-start.11 = (s32[1,64]{1,0:T(1,128)S(1)}, s32[1,64]{1,0:T(1,128)}, u32[]{:S(2)}) copy-start(s32[1,64]{1,0:T(1,128)} %owner_ref.1) | copy-start | bytes 772
  167.5 3.3 %copy-start.12 = (s32[1,64]{1,0:T(1,128)S(1)}, s32[1,64]{1,0:T(1,128)}, u32[]{:S(2)}) copy-start(s32[1,64]{1,0:T(1,128)} %block_ref.1) | copy-start | bytes 772
